TPU v7x, 128 devices: a whole 4x4x4 slice. The times are simulated.
128 devices in a mesh: row: 16 (over x, y), col: 8 (over z, core).
Axes of the slice: x: 4, y: 4, z: 4, core: 2. Of those that a mesh axis runs over, the one named last changes fastest.
Arguments:
- source_points: bfloat16 [65536, 1024], P('row'), may hold values from -8 to 8
- target_points: bfloat16 [32768, 1024], P('col', 'row'), may hold values from -8 to 8
- source_mass: float32 [65536], P('row'), may hold values from 0.25 to 4
- target_mass: float32 [32768], P('col'), may hold values from 0.25 to 4
- tile_index: int32 [256, 16], P('row', 'col'), may hold values from 0 to 15, as said below
- tile_count: int32 [256, 8], P('row', 'col'), may hold values from 1 to 2, as said below
Outputs:
- source_potential: float32 [65536], P('row')
- target_potential: float32 [32768], P('col')
Inputs may be any that keep to these rules, and one draw needn't show every extreme that they name: `tile_index`: within the 2 slots of one source tile and one index of col the target tiles are distinct; every target tile is named by a live slot of some source tile. `tile_count`: each index of row holds, for every index of col, a source tile with all 2 slots live.
All inputs are finite; a program needn't handle non-finite values.
Results may differ from a plain program's by a relative error of at most 0.0003.
Values may be sent and summed in bfloat16 or wider, within the bound.
A program may use at most 128 MiB of HBM per device.

v0:
```python
import math
import jax
import jax.numpy as jnp
from jax import lax
from jax.sharding import PartitionSpec as P

TILE = 256
ITERS = 3
masked_score = -1e30


def cost_terms(piece, source_points, tile_index):
    width = piece.shape[1]
    source_tiles = source_points.reshape(-1, TILE, width)
    target_tiles = piece.reshape(-1, TILE, width)
    chosen = target_tiles[tile_index]
    return jnp.einsum("rad,rkbd->rkab", source_tiles, chosen, preferred_element_type=jnp.float32)


def on_device(source_points, target_points, source_mass, target_mass, tile_index, tile_count):
    tiles_per_row = source_points.shape[0] // TILE
    col_tiles = target_points.shape[0] // TILE
    slot_count = tile_index.shape[1]
    scale = 1.0 / math.sqrt(source_points.shape[1])
    live = jnp.arange(slot_count)[None, :] < tile_count
    onehot = (tile_index[:, :, None] == jnp.arange(col_tiles)[None, None, :]) & live[:, :, None]
    log_source = jnp.log(source_mass).reshape(tiles_per_row, TILE)
    log_target = jnp.log(target_mass).reshape(col_tiles, TILE)
    target_pot = jnp.zeros((col_tiles, TILE), jnp.float32)
    source_pot = jnp.zeros((tiles_per_row, TILE), jnp.float32)
    for iteration in range(ITERS):
        cost = (
            cost_terms(
                lax.all_gather(target_points, "row", axis=1, tiled=True), source_points, tile_index
            )
            * scale
        )
        scores = cost + target_pot[tile_index][:, :, None, :]
        scores = jnp.where(live[:, :, None, None], scores, masked_score)
        row_top = jnp.max(scores, axis=(1, 3))
        highest = lax.pmax(row_top, "col")
        local_sum = jnp.sum(jnp.exp(scores - highest[:, None, :, None]), axis=(1, 3))
        total = lax.psum(local_sum, "col")
        source_pot = log_source - highest - jnp.log(total)
        columns = cost + source_pot[:, None, :, None]
        columns = jnp.where(live[:, :, None, None], columns, masked_score)
        slot_top = jnp.max(columns, axis=2)
        local_top = jnp.max(
            jnp.where(onehot[..., None], slot_top[:, :, None, :], masked_score), axis=(0, 1)
        )
        col_high = lax.pmax(local_top, "row")
        slot_ref = col_high[tile_index]
        sums = jnp.sum(jnp.exp(columns - slot_ref[:, :, None, :]), axis=2)
        col_sum = jnp.sum(jnp.where(onehot[..., None], sums[:, :, None, :], 0.0), axis=(0, 1))
        col_total = lax.psum(col_sum, "row")
        target_pot = log_target - col_high - jnp.log(col_total)
    return (source_pot.reshape(-1), target_pot.reshape(-1))


def solution(mesh):
    placed = (P("row", None), P("col", "row"), P("row"), P("col"), P("row", "col"), P("row", "col"))
    return jax.shard_map(
        on_device, mesh=mesh, in_specs=placed, out_specs=(P("row"), P("col")), check_vma=False
    )
```

profile of v0, /device:TPU:0, one launch (start us, length us, event | category | flops | bytes accessed | tf_op | source)
XLA Modules:
  0.0 747.5 jit_solution(9227641684370280702)
XLA Ops:
  12.5 70.8 %all-gather.2.cloned.1.call-done = bf16[4096,1024]{0,1:T(8,128)(2,1)} async-done(((bf16[4096,64]{0,1:T(8,128)(2,1)}), bf16[4096,1024]{0,1:T(8,128)(2,1)}) %all-gather.2.cloned.1.call-update) | async-done | bytes 8388624 | tf_op jit(solution)/shard_map/all_gather | solution.py:34
  83.2 12.0 %copy.14 = bf16[4096,1024]{1,0:T(8,128)(2,1)} copy(bf16[4096,1024]{0,1:T(8,128)(2,1)} %all-gather.2.cloned.1.call-done) | data formatting | bytes 16777216 | tf_op jit(solution)/shard_map/all_gather | solution.py:34
  95.2 10.6 %gather_fusion = bf16[32,256,1024]{2,1,0:T(8,128)(2,1)} fusion(bf16[16,256,1024]{2,1,0:T(8,128)(2,1)} %bitcast.57, s32[1024]{0:T(1024)S(1)} %pad_clamp_fusion), kind=kCustom, calls=%fused_computation | custom fusion | bytes 33554560 | tf_op jit(solution)/shard_map/gather | solution.py:16
  105.8 13.5 %bitcast_reduce_fusion.5 = (f32[16,256]{1,0:T(8,128)S(1)}, f32[16,2,256,256]{3,2,1,0:T(8,128)}) fusion(f32[16,2,256]{2,1,0:T(2,128)S(1)} %reshape.108, pred[16,2]{1,0:T(8,128)(4,1)S(1)} %iota_compare_fusion, bf16[16,2,256,1024]{3,2,1,0:T(8,128)(2,1)} %bitcast.58, bf16[16,256,1024,1]{2,1,3,0:T(8,128)(2,1)} %bitcast.63), kind=kOutput, calls=%fused_computation.28 | convolution fusion | flops 4303351808 | bytes 33603616 | tf_op jit(solution)/shard_map/rad,rkbd->rkab/dot_general | solution.py:17
  119.3 25.8 %pmax.42 = f32[16,256]{1,0:T(8,128)S(1)} all-reduce(f32[16,256]{1,0:T(8,128)S(1)} %get-tuple-element.2), channel_id=1, replica_groups=mesh['row'=16,'col'=8] {'col'}, use_global_device_ids=true, to_apply=%region_1.2 | all-reduce | flops 4096 | bytes 32768 | tf_op jit(solution)/shard_map/pmax | solution.py:41
  145.1 4.6 fusion.11
  149.8 23.6 %psum.42 = f32[16,256]{1,0:T(8,128)S(1)} all-reduce(f32[16,256]{1,0:T(8,128)S(1)} %fusion.11), channel_id=1, replica_groups=mesh['row'=16,'col'=8] {'col'}, use_global_device_ids=true, to_apply=%region_3.4 | all-reduce | flops 4096 | bytes 32768 | tf_op jit(solution)/shard_map/psum | solution.py:43
  173.3 4.7 bitcast_reduce_fusion.4
  178.1 72.4 %pmax.43 = f32[16,256]{1,0:T(8,128)S(1)} all-reduce(f32[16,256]{1,0:T(8,128)S(1)} %select_reduce_fusion.5), channel_id=1, replica_groups=mesh['row'=16,'col'=8] {'row'}, use_global_device_ids=true, to_apply=%region_6.7 | all-reduce | flops 4096 | bytes 32768 | tf_op jit(solution)/shard_map/pmax | solution.py:51
  251.1 5.1 fusion.9
  256.4 69.5 %psum.43 = f32[16,256]{1,0:T(8,128)S(1)} all-reduce(f32[16,256]{1,0:T(8,128)S(1)} %select_reduce_fusion.4), channel_id=1, replica_groups=mesh['row'=16,'col'=8] {'row'}, use_global_device_ids=true, to_apply=%region_9.10 | all-reduce | flops 4096 | bytes 32768 | tf_op jit(solution)/shard_map/psum | solution.py:55
  331.0 23.7 %pmax.44 = f32[16,256]{1,0:T(8,128)S(1)} all-reduce(f32[16,256]{1,0:T(8,128)S(1)} %bitcast_reduce_fusion.3), channel_id=1, replica_groups=mesh['row'=16,'col'=8] {'col'}, use_global_device_ids=true, to_apply=%region_11.12 | all-reduce | flops 4096 | bytes 32768 | tf_op jit(solution)/shard_map/pmax | solution.py:41
  354.8 4.6 fusion.7
  359.4 23.6 %psum.44 = f32[16,256]{1,0:T(8,128)S(1)} all-reduce(f32[16,256]{1,0:T(8,128)S(1)} %fusion.7), channel_id=1, replica_groups=mesh['row'=16,'col'=8] {'col'}, use_global_device_ids=true, to_apply=%region_13.14 | all-reduce | flops 4096 | bytes 32768 | tf_op jit(solution)/shard_map/psum | solution.py:43
  383.0 4.7 bitcast_reduce_fusion.2
  387.8 69.5 %pmax.45 = f32[16,256]{1,0:T(8,128)S(1)} all-reduce(f32[16,256]{1,0:T(8,128)S(1)} %select_reduce_fusion.3), channel_id=1, replica_groups=mesh['row'=16,'col'=8] {'row'}, use_global_device_ids=true, to_apply=%region_16.17 | all-reduce | flops 4096 | bytes 32768 | tf_op jit(solution)/shard_map/pmax | solution.py:51
  458.0 5.1 fusion.5
  463.2 69.5 %psum.45 = f32[16,256]{1,0:T(8,128)S(1)} all-reduce(f32[16,256]{1,0:T(8,128)S(1)} %select_reduce_fusion.2), channel_id=1, replica_groups=mesh['row'=16,'col'=8] {'row'}, use_global_device_ids=true, to_apply=%region_19.20 | all-reduce | flops 4096 | bytes 32768 | tf_op jit(solution)/shard_map/psum | solution.py:55
  537.8 23.6 %pmax.46 = f32[16,256]{1,0:T(8,128)S(1)} all-reduce(f32[16,256]{1,0:T(8,128)S(1)} %bitcast_reduce_fusion.1), channel_id=1, replica_groups=mesh['row'=16,'col'=8] {'col'}, use_global_device_ids=true, to_apply=%region_21.22 | all-reduce | flops 4096 | bytes 32768 | tf_op jit(solution)/shard_map/pmax | solution.py:41
  566.0 23.6 %psum.46 = f32[16,256]{1,0:T(8,128)S(1)} all-reduce(f32[16,256]{1,0:T(8,128)S(1)} %fusion.3), channel_id=1, replica_groups=mesh['row'=16,'col'=8] {'col'}, use_global_device_ids=true, to_apply=%region_23.24 | all-reduce | flops 4096 | bytes 32768 | tf_op jit(solution)/shard_map/psum | solution.py:43
  589.6 4.7 bitcast_reduce_fusion
  594.4 69.5 %pmax.47 = f32[16,256]{1,0:T(8,128)S(1)} all-reduce(f32[16,256]{1,0:T(8,128)S(1)} %select_reduce_fusion.1), channel_id=1, replica_groups=mesh['row'=16,'col'=8] {'row'}, use_global_device_ids=true, to_apply=%region_26.27 | all-reduce | flops 4096 | bytes 32768 | tf_op jit(solution)/shard_map/pmax | solution.py:51
  664.6 5.1 fusion.1
  669.8 69.5 %psum.47 = f32[16,256]{1,0:T(8,128)S(1)} all-reduce(f32[16,256]{1,0:T(8,128)S(1)} %select_reduce_fusion), channel_id=1, replica_groups=mesh['row'=16,'col'=8] {'row'}, use_global_device_ids=true, to_apply=%region_29.30 | all-reduce | flops 4096 | bytes 32768 | tf_op jit(solution)/shard_map/psum | solution.py:55
  (43 shorter events, 24.0 us)
Async XLA Ops:
  7.2 76.1 %all-gather.2.cloned.1.call-start = ((), (), s32[]{:S(2)}) async-start(), calls=%async_computation | async-start | bytes 8912896 | tf_op jit(solution)/shard_map/all_gather | solution.py:34
Sparse Core Ops, SparseCore 0:
  10.1 73.0 all-gather.1
where the time goes:
time: 748 us; the launch traced here: 747 us
  blocking collectives  564 us (75%)
  waiting for transfers between devices  71.4 us (10%)
  other arithmetic  54.5 us (7%)
  local copies, waits for them, and re-layouts  30 us (4%)
  between operations  14.3 us (2%)
  matrix products  13.5 us (2%)
    pmax x3, blocking collectives, on_device(): col_high = lax.pmax(local_top, 'row')  211 us
    psum x3, blocking collectives, on_device(): col_total = lax.psum(col_sum, 'row')  209 us
    pmax x3, blocking collectives, on_device(): highest = lax.pmax(row_top, 'col')  73.1 us
    all_gather x1, waiting for transfers between devices, on_device(): lax.all_gather(target_points, 'row', axis=1, tiled=True)  70.8 us
    psum x3, blocking collectives, on_device(): total = lax.psum(local_sum, 'col')  70.7 us
    reduce_sum x3, other arithmetic, on_device(): sums = jnp.sum(jnp.exp(columns - slot_ref[:, :, None, :]), axis=2)  15.4 us
  transfers between devices with their start and end apart: 1, of which 1 were waited for; matrix products, arithmetic and copies ran while one was open for 1% of the time, Pallas kernels for 0%

commit v1 on v0

--- a/solution.py
+++ b/solution.py
@@ -3,6 +3,7 @@
 import jax.numpy as jnp
 from jax import lax
 from jax.sharding import PartitionSpec as P
+from jax.lax import all_to_all, axis_size
 
 TILE = 256
 ITERS = 3
@@ -29,11 +30,20 @@
     target_pot = jnp.zeros((col_tiles, TILE), jnp.float32)
     source_pot = jnp.zeros((tiles_per_row, TILE), jnp.float32)
     for iteration in range(ITERS):
+
+        def recover_the_shifts_all(arr, k_dim):
+            return jnp.concatenate(
+                all_to_all(
+                    jnp.stack([arr] * axis_size("row"), 0),
+                    split_axis=0,
+                    axis_name="row",
+                    concat_axis=0,
+                ),
+                k_dim,
+            )
+
         cost = (
-            cost_terms(
-                lax.all_gather(target_points, "row", axis=1, tiled=True), source_points, tile_index
-            )
-            * scale
+            cost_terms(recover_the_shifts_all(target_points, 1), source_points, tile_index) * scale
         )
         scores = cost + target_pot[tile_index][:, :, None, :]
         scores = jnp.where(live[:, :, None, None], scores, masked_score)

time: 748 us -> 827 us (1.11)
  waiting for transfers between devices: 71.4 us -> 146 us
  between operations: 14.3 us -> 0.95 us
  local copies, waits for them, and re-layouts: 30 us -> 43.2 us
    all_to_all x0 -> x1, waiting for transfers between devices: none -> 146 us  [recover_the_shifts_all(): all_to_all(jnp.stack([arr] * axis_size('row'), 0), split_axis=0, axis_nam...]
    all_gather x1 -> x0, waiting for transfers between devices: 70.8 us -> none  [on_device(): lax.all_gather(target_points, 'row', axis=1, tiled=True)]
    another operation x0 -> x2, local copies, waits for them, and re-layouts: none -> 17.6 us  [the longest x1 12.2 us: cost_terms(): target_tiles = piece.reshape(-1, TILE, width)]
    all_gather x1 -> x0, local copies, waits for them, and re-layouts: 12 us -> none  [on_device(): lax.all_gather(target_points, 'row', axis=1, tiled=True)]
    unnamed x3 -> x12, local copies, waits for them, and re-layouts: 1.99 us -> 11 us
  transfers between devices with their start and end apart: 1 -> 1, of which waited for: 1 -> 1; matrix products, arithmetic and copies ran while one was open for 1% -> 0% of each run, Pallas kernels for 0% -> 0%
where the time goes in v1:
time: 827 us; the launch traced here: 826 us
  blocking collectives  561 us (68%)
  waiting for transfers between devices  146 us (18%)
  other arithmetic  53.2 us (6%)
  local copies, waits for them, and re-layouts  43.2 us (5%)
  matrix products  13.5 us (2%)
    pmax x3, blocking collectives, on_device(): col_high = lax.pmax(local_top, 'row')  210 us
    psum x3, blocking collectives, on_device(): col_total = lax.psum(col_sum, 'row')  209 us
    all_to_all x1, waiting for transfers between devices, recover_the_shifts_all(): all_to_all(jnp.stack([arr] * axis_size('row'), 0), split_axis=0, axis_nam...  146 us
    pmax x3, blocking collectives, on_device(): highest = lax.pmax(row_top, 'col')  72.2 us
    psum x3, blocking collectives, on_device(): total = lax.psum(local_sum, 'col')  70.9 us
  transfers between devices with their start and end apart: 1, of which 1 were waited for; matrix products, arithmetic and copies ran while one was open for 0% of the time, Pallas kernels for 0%

profile of v1, /device:TPU:0, one launch (start us, length us, event | category | flops | bytes accessed | tf_op | source)
XLA Modules:
  0.0 826.0 jit_solution(9180183259429362478)
XLA Ops:
  0.6 5.3 stack.2
  6.0 7.3 all-to-all-start
  14.5 146.5 %all-to-all-done = bf16[16,4096,64]{1,2,0:T(8,128)(2,1)} async-done(((bf16[16,4096,64]{1,2,0:T(8,128)(2,1)}), bf16[16,4096,64]{1,2,0:T(8,128)(2,1)}, u32[]{:S(2)}, u32[]{:S(2)}) %all-to-all-start) | async-done | bytes 8388640 | tf_op jit(solution)/shard_map/all_to_all | solution.py:36
  160.9 9.7 %copy.21 = bf16[128,8,16,256]{3,2,1,0:T(8,128)(2,1)} copy(bf16[128,8,16,256]{3,1,2,0:T(8,128)(2,1)} %bitcast.16) | data formatting | bytes 16777216
  170.6 12.2 %copy.18 = bf16[16,256,1024]{2,1,0:T(8,128)(2,1)} copy(bf16[16,256,1024]{1,0,2:T(8,128)(2,1)} %bitcast.62) | data formatting | bytes 16777216 | tf_op jit(solution)/shard_map/reshape;reshape | solution.py:16
  182.9 10.6 %gather_fusion = bf16[32,256,1024]{2,1,0:T(8,128)(2,1)} fusion(bf16[16,256,1024]{2,1,0:T(8,128)(2,1)} %copy.18, s32[1024]{0:T(1024)S(1)} %pad_clamp_fusion), kind=kCustom, calls=%fused_computation | custom fusion | bytes 33554560 | tf_op jit(solution)/shard_map/gather | solution.py:17
  193.5 13.5 %bitcast_reduce_fusion.5 = (f32[16,256]{1,0:T(8,128)S(1)}, f32[16,2,256,256]{3,2,1,0:T(8,128)}) fusion(f32[16,2,256]{2,1,0:T(2,128)S(1)} %reshape.110, pred[16,2]{1,0:T(8,128)(4,1)S(1)} %iota_compare_fusion, bf16[16,2,256,1024]{3,2,1,0:T(8,128)(2,1)} %bitcast.63, bf16[16,256,1024,1]{2,1,3,0:T(8,128)(2,1)} %bitcast.68), kind=kOutput, calls=%fused_computation.28 | convolution fusion | flops 4303351808 | bytes 33603616 | tf_op jit(solution)/shard_map/rad,rkbd->rkab/dot_general | solution.py:18
  207.0 25.1 %pmax.42 = f32[16,256]{1,0:T(8,128)S(1)} all-reduce(f32[16,256]{1,0:T(8,128)S(1)} %get-tuple-element.2), channel_id=1, replica_groups=mesh['row'=16,'col'=8] {'col'}, use_global_device_ids=true, to_apply=%region_1.2 | all-reduce | flops 4096 | bytes 32768 | tf_op jit(solution)/shard_map/pmax | solution.py:51
  236.7 23.6 %psum.42 = f32[16,256]{1,0:T(8,128)S(1)} all-reduce(f32[16,256]{1,0:T(8,128)S(1)} %fusion.11), channel_id=1, replica_groups=mesh['row'=16,'col'=8] {'col'}, use_global_device_ids=true, to_apply=%region_3.4 | all-reduce | flops 4096 | bytes 32768 | tf_op jit(solution)/shard_map/psum | solution.py:53
  260.3 4.7 bitcast_reduce_fusion.4
  265.1 70.8 %pmax.43 = f32[16,256]{1,0:T(8,128)S(1)} all-reduce(f32[16,256]{1,0:T(8,128)S(1)} %select_reduce_fusion.5), channel_id=1, replica_groups=mesh['row'=16,'col'=8] {'row'}, use_global_device_ids=true, to_apply=%region_6.7 | all-reduce | flops 4096 | bytes 32768 | tf_op jit(solution)/shard_map/pmax | solution.py:61
  336.5 5.1 fusion.9
  341.8 69.5 %psum.43 = f32[16,256]{1,0:T(8,128)S(1)} all-reduce(f32[16,256]{1,0:T(8,128)S(1)} %select_reduce_fusion.4), channel_id=1, replica_groups=mesh['row'=16,'col'=8] {'row'}, use_global_device_ids=true, to_apply=%region_9.10 | all-reduce | flops 4096 | bytes 32768 | tf_op jit(solution)/shard_map/psum | solution.py:65
  416.4 23.6 %pmax.44 = f32[16,256]{1,0:T(8,128)S(1)} all-reduce(f32[16,256]{1,0:T(8,128)S(1)} %bitcast_reduce_fusion.3), channel_id=1, replica_groups=mesh['row'=16,'col'=8] {'col'}, use_global_device_ids=true, to_apply=%region_11.12 | all-reduce | flops 4096 | bytes 32768 | tf_op jit(solution)/shard_map/pmax | solution.py:51
  444.6 23.6 %psum.44 = f32[16,256]{1,0:T(8,128)S(1)} all-reduce(f32[16,256]{1,0:T(8,128)S(1)} %fusion.7), channel_id=1, replica_groups=mesh['row'=16,'col'=8] {'col'}, use_global_device_ids=true, to_apply=%region_13.14 | all-reduce | flops 4096 | bytes 32768 | tf_op jit(solution)/shard_map/psum | solution.py:53
  473.0 69.5 %pmax.45 = f32[16,256]{1,0:T(8,128)S(1)} all-reduce(f32[16,256]{1,0:T(8,128)S(1)} %select_reduce_fusion.3), channel_id=1, replica_groups=mesh['row'=16,'col'=8] {'row'}, use_global_device_ids=true, to_apply=%region_16.17 | all-reduce | flops 4096 | bytes 32768 | tf_op jit(solution)/shard_map/pmax | solution.py:61
  543.1 5.1 fusion.5
  548.4 69.5 %psum.45 = f32[16,256]{1,0:T(8,128)S(1)} all-reduce(f32[16,256]{1,0:T(8,128)S(1)} %select_reduce_fusion.2), channel_id=1, replica_groups=mesh['row'=16,'col'=8] {'row'}, use_global_device_ids=true, to_apply=%region_19.20 | all-reduce | flops 4096 | bytes 32768 | tf_op jit(solution)/shard_map/psum | solution.py:65
  623.0 23.6 %pmax.46 = f32[16,256]{1,0:T(8,128)S(1)} all-reduce(f32[16,256]{1,0:T(8,128)S(1)} %bitcast_reduce_fusion.1), channel_id=1, replica_groups=mesh['row'=16,'col'=8] {'col'}, use_global_device_ids=true, to_apply=%region_21.22 | all-reduce | flops 4096 | bytes 32768 | tf_op jit(solution)/shard_map/pmax | solution.py:51
  651.2 23.8 %psum.46 = f32[16,256]{1,0:T(8,128)S(1)} all-reduce(f32[16,256]{1,0:T(8,128)S(1)} %fusion.3), channel_id=1, replica_groups=mesh['row'=16,'col'=8] {'col'}, use_global_device_ids=true, to_apply=%region_23.24 | all-reduce | flops 4096 | bytes 32768 | tf_op jit(solution)/shard_map/psum | solution.py:53
  675.0 4.7 bitcast_reduce_fusion
  679.8 69.5 %pmax.47 = f32[16,256]{1,0:T(8,128)S(1)} all-reduce(f32[16,256]{1,0:T(8,128)S(1)} %select_reduce_fusion.1), channel_id=1, replica_groups=mesh['row'=16,'col'=8] {'row'}, use_global_device_ids=true, to_apply=%region_26.27 | all-reduce | flops 4096 | bytes 32768 | tf_op jit(solution)/shard_map/pmax | solution.py:61
  750.0 5.1 fusion.1
  755.2 69.5 %psum.47 = f32[16,256]{1,0:T(8,128)S(1)} all-reduce(f32[16,256]{1,0:T(8,128)S(1)} %select_reduce_fusion), channel_id=1, replica_groups=mesh['row'=16,'col'=8] {'row'}, use_global_device_ids=true, to_apply=%region_29.30 | all-reduce | flops 4096 | bytes 32768 | tf_op jit(solution)/shard_map/psum | solution.py:65
  (52 shorter events, 33.8 us)
Async XLA Ops:
  6.0 7.3 copy-start.2
  6.0 8.3 %copy-start = (f32[4096]{0:T(1024)S(1)}, f32[4096]{0:T(1024)}, u32[]{:S(2)}) copy-start(f32[4096]{0:T(1024)} %param.8) | copy-start | bytes 49156
  6.0 8.3 %copy-start.1 = (f32[4096]{0:T(1024)S(1)}, f32[4096]{0:T(1024)}, u32[]{:S(2)}) copy-start(f32[4096]{0:T(1024)} %param.9) | copy-start | bytes 49156
  6.0 8.3 %copy-start.3 = (s32[16,1]{0,1:T(1,128)S(1)}, s32[16,1]{0,1:T(1,128)}, u32[]{:S(2)}) copy-start(s32[16,1]{0,1:T(1,128)} %param.11) | copy-start | bytes 196
  6.0 155.0 %all-to-all-start = ((bf16[16,4096,64]{1,2,0:T(8,128)(2,1)}), bf16[16,4096,64]{1,2,0:T(8,128)(2,1)}, u32[]{:S(2)}, u32[]{:S(2)}) async-start(bf16[16,4096,64]{1,2,0:T(8,128)(2,1)} %stack.2), calls=%async_computation | async-start | bytes 16777216 | tf_op jit(solution)/shard_map/all_to_all | solution.py:36
